TPU v7x, 32 devices: a whole 2x2x4 slice. The times are simulated.
32 devices in a mesh: phi: 8 (over z, core), mom: 4 (over y, x).
Axes of the slice: x: 2, y: 2, z: 4, core: 2. Of those that a mesh axis runs over, the one named last changes fastest.
Arguments:
- spectra: float32 [32, 4, 16, 64, 256], P('mom', None, 'phi'), may hold values from 0.1 to 3
- production: bfloat16 [32, 32], replicated, may hold values from 0 to 0.119628906
- bin_group: int32 [32], replicated, may hold values from 0 to 3
- parent_of: int32 [4], replicated, may hold values from 0 to 3
- diffusivity: float32 [64, 256], replicated, may hold values from 0.05 to 0.22
- height_inverse: float32 [64, 64], replicated, may hold values from -1 to 1, as said below
- loss_rate: float32 [32], P('mom'), may hold values from 2 to 20
- density: float32 [16, 64, 256], P('phi'), may hold values from 0.5 to 2
Outputs:
- spectra_out: float32 [32, 4, 16, 64, 256], P('mom', None, 'phi')
Inputs may be any that keep to these rules, and one draw needn't show every extreme that they name: `height_inverse`: diagonal entries lie between 0.7 and 1, off-diagonal entries are small.
All inputs are finite; a program needn't handle non-finite values.
Results may differ from a plain program's by a relative error of at most 0.00085.
Values may be sent and summed in bfloat16 or wider, within the bound.
A program may use at most 64 MiB of HBM per device.

v0:
```python
import functools
import math

import jax
import jax.numpy as jnp
from jax import lax
from jax.experimental import pallas as pl
from jax.experimental.pallas import tpu as pltpu
from jax.sharding import PartitionSpec as P

MESH = pl.DeviceIdType.MESH
ROWS = 16


def grid_of(count):
    columns = max(d for d in range(1, math.isqrt(count) + 1) if count % d == 0)
    return count // columns, columns


def dot(a, b):
    return jnp.dot(a, b, preferred_element_type=jnp.float32)


def dot_nt(a, b):
    return lax.dot_general(a, b, (((1,), (1,)), ((), ())), preferred_element_type=jnp.float32)


def onehot_bins(first_bins, bins, total):
    local = lax.broadcasted_iota(jnp.int32, (bins, ROWS, total), 0)
    whole = lax.broadcasted_iota(jnp.int32, (bins, ROWS, total), 2)
    parts = [
        jnp.where(local + first == whole, 1.0, 0.0).reshape(bins * ROWS, total)
        for first in first_bins
    ]
    return jnp.concatenate(parts, axis=0).astype(jnp.bfloat16)


def step_kernel(
    ny,
    nx,
    f_hbm,
    kernel_ref,
    parent_hbm,
    diff_hbm,
    inverse_hbm,
    rate_hbm,
    density_hbm,
    settled_ref,
    hin,
    weight,
    f_ref,
    parent_ref,
    diff_ref,
    inverse_ref,
    rate_ref,
    density_ref,
    comb,
    psend,
    precv,
    acc,
    faces_out,
    faces_in,
    below,
    above,
    hout,
    keep,
    rates_out,
    rates_in,
    wide_0,
    wide_1,
    height,
    coef,
    in_sem,
    out_sem,
    x_send,
    x_recv,
    y_send,
    y_recv,
    f_send,
    f_recv,
    a_send,
    a_recv,
    h_send,
    h_recv,
    r_send,
    r_recv,
):
    bins, species, cells, heights, radii = f_ref.shape
    total_bins = kernel_ref.shape[0]
    count = ny * nx
    wides = (wide_0, wide_1)
    phi = lax.axis_index("phi")
    mom = lax.axis_index("mom")
    phis = lax.axis_size("phi")
    row, col = mom // nx, mom % nx
    right, left = (phi + 1) % phis, (phi + phis - 1) % phis

    load = pltpu.make_async_copy(f_hbm, f_ref, in_sem.at[0])
    small = [
        pltpu.make_async_copy(parent_hbm, parent_ref, in_sem.at[1]),
        pltpu.make_async_copy(rate_hbm, rate_ref, in_sem.at[2]),
        pltpu.make_async_copy(diff_hbm, diff_ref, in_sem.at[3]),
        pltpu.make_async_copy(inverse_hbm, inverse_ref, in_sem.at[4]),
        pltpu.make_async_copy(density_hbm, density_ref, in_sem.at[5]),
    ]
    small[0].start()
    load.start()
    for copy in small[1:]:
        copy.start()
    barrier = pltpu.get_barrier_semaphore()
    for d in range(1, count):
        pl.semaphore_signal(
            barrier, inc=1, device_id={"mom": (mom + d) % count}, device_id_type=MESH
        )
    for side in (left, right):
        pl.semaphore_signal(barrier, inc=1, device_id={"phi": side}, device_id_type=MESH)

    def along_row(d):
        return {"mom": row * nx + (col + d) % nx}

    def along_col(e):
        return {"mom": ((row + e) % ny) * nx + col}

    def sizes(x):
        return (nx, ny) if x % 2 == 0 else (ny, nx)

    def parent_copy(s, x, d):
        c = s * cells + x
        return pltpu.make_async_remote_copy(
            src_ref=comb.at[c, 0],
            dst_ref=comb.at[c, d],
            send_sem=x_send.at[c, d - 1],
            recv_sem=x_recv.at[c, d - 1],
            device_id=along_row(d) if x % 2 == 0 else along_col(d),
            device_id_type=MESH,
        )

    def partial_copy(s, x, e):
        c = s * cells + x
        return pltpu.make_async_remote_copy(
            src_ref=psend.at[c, e - 1],
            dst_ref=precv.at[c, e - 1],
            send_sem=y_send.at[c, e - 1],
            recv_sem=y_recv.at[c, e - 1],
            device_id=along_col(e) if x % 2 == 0 else along_row(e),
            device_id_type=MESH,
        )

    def face_copy(s, side):
        return pltpu.make_async_remote_copy(
            src_ref=faces_out.at[s, side],
            dst_ref=faces_in.at[s, side],
            send_sem=f_send.at[s, side],
            recv_sem=f_recv.at[s, side],
            device_id={"phi": left if side == 0 else right},
            device_id_type=MESH,
        )

    def below_copy(s):
        return pltpu.make_async_remote_copy(
            src_ref=below.at[s],
            dst_ref=above.at[s],
            send_sem=a_send.at[s],
            recv_sem=a_recv.at[s],
            device_id={"mom": (mom + count - 1) % count},
            device_id_type=MESH,
        )

    def h_copy(s, k):
        return pltpu.make_async_remote_copy(
            src_ref=hout.at[s],
            dst_ref=hin.at[s],
            send_sem=h_send.at[s, k],
            recv_sem=h_recv.at[s],
            device_id={"mom": (mom + count - 1 - k) % count},
            device_id_type=MESH,
        )

    def rate_copy():
        return pltpu.make_async_remote_copy(
            src_ref=rates_out,
            dst_ref=rates_in,
            send_sem=r_send,
            recv_sem=r_recv,
            device_id={"mom": (mom + count - 1) % count},
            device_id_type=MESH,
        )

    def settled_copy(s):
        part = pl.ds(s * cells, cells)
        return pltpu.make_async_copy(acc.at[part], settled_ref.at[part], out_sem.at[s])

    def fill_parents(s):
        parent = parent_ref[s]
        for x in range(cells):
            for q in range(bins):
                comb[s * cells + x, 0, q] = f_ref[q, parent, x].astype(jnp.bfloat16)

    def send_parents(s):
        for x in range(cells):
            for d in range(1, sizes(x)[0]):
                parent_copy(s, x, d).start()

    odd = mom % 2 == 1
    ahead = 2
    small[0].wait()
    load.wait()
    fill_parents(0)
    pl.semaphore_wait(barrier, count + 1)
    send_parents(0)

    @pl.loop(1, species)
    def _(s):
        fill_parents(s)

        @pl.when(s < ahead)
        def _():
            send_parents(s)

    for copy in small[1:]:
        copy.wait()
    for p in range(bins):
        rates_out[p] = jnp.full((8, radii), rate_ref[p], jnp.float32)

    @pl.when(odd)
    def _():
        rate_copy().start()

    row_starts = [(row * nx + (col + d) % nx) * bins for d in range(nx)]
    col_starts = [(((row + e) % ny) * nx + col) * bins for e in range(ny)]
    row_froms = [(row * nx + (col + nx - d) % nx) * bins for d in range(nx)]
    col_froms = [(((row + ny - e) % ny) * nx + col) * bins for e in range(ny)]
    for to, source_from, ref in ((col_starts, row_froms, wide_0), (row_starts, col_froms, wide_1)):
        rows_1h = onehot_bins(to, bins, total_bins)
        cols_1h = onehot_bins(source_from, bins, total_bins)
        mixed = dot_nt(dot(rows_1h, kernel_ref[...]).astype(jnp.bfloat16), cols_1h)
        r_at = lax.broadcasted_iota(jnp.int32, mixed.shape, 0) & (ROWS - 1)
        c_at = lax.broadcasted_iota(jnp.int32, mixed.shape, 1) & (ROWS - 1)
        ref[...] = jnp.where(r_at == c_at, mixed, 0.0).astype(jnp.bfloat16)

    group = height.shape[1] // heights
    a_at = lax.broadcasted_iota(jnp.int32, (heights, heights), 0)
    b_at = lax.broadcasted_iota(jnp.int32, (heights, heights), 1)
    stencil = jnp.where(a_at == b_at, 0.5, 0.0) + jnp.where(jnp.abs(a_at - b_at) == 1, 0.25, 0.0)
    both = jnp.dot(
        inverse_ref[...],
        stencil,
        precision=lax.Precision.HIGHEST,
        preferred_element_type=jnp.float32,
    )
    high = both.astype(jnp.bfloat16).astype(jnp.float32)
    tall_a = lax.broadcasted_iota(jnp.int32, (group, heights, heights), 1)
    tall_b = lax.broadcasted_iota(jnp.int32, (group, heights, heights), 2)
    spread = jnp.where(tall_a == tall_b, 1.0, 0.0).reshape(group * heights, heights)
    spread = spread.astype(jnp.bfloat16)
    row_g = lax.broadcasted_iota(jnp.int32, (group, heights, group * heights), 0)
    col_g = lax.broadcasted_iota(jnp.int32, (group, heights, group * heights), 2)
    first = row_g * heights
    inside = jnp.where((col_g >= first) & (col_g < first + heights), 1.0, 0.0)
    inside = inside.reshape(group * heights, group * heights)
    for k, part in enumerate((high, both - high)):
        tall = jnp.concatenate([part] * group, axis=0).astype(jnp.bfloat16)
        height[k] = (dot_nt(tall, spread) * inside).astype(jnp.bfloat16)

    diff = diff_ref[...]
    lane = lax.broadcasted_iota(jnp.int32, diff.shape, 1)
    coef[0] = 1.0 - 3.0 * diff
    coef[1] = jnp.where(lane == 0, 0.0, 0.5 * diff)
    coef[2] = jnp.where(lane == radii - 1, 0.0, 0.5 * diff)

    for x in range(cells):
        kept = jnp.ones((heights, radii), jnp.float32)
        for p in range(bins):
            part = 1.0 / (1.0 + 0.5 * rate_ref[p] * density_ref[x])
            weight[p, x] = part
            kept = kept * (1.0 - part)
        keep[0, x] = kept

    def keep_above():
        rate_copy().wait_recv()
        for x in range(cells):
            kept = jnp.ones((heights // 8, 8, radii), jnp.float32)
            dens = density_ref[x].reshape(heights // 8, 8, radii)
            for p in range(bins):
                kept = kept * (1.0 - 1.0 / (1.0 + 0.5 * rates_in[p] * dens))
            keep[1, x] = kept.reshape(heights, radii)

    @pl.when(mom >= count - 2)
    def _():
        hin[...] = jnp.zeros_like(hin)

    def mix(s):
        for x in range(cells):
            c = s * cells + x
            n1, n2 = sizes(x)
            for d in range(1, n1):
                parent_copy(s, x, d).wait_recv()

            @pl.loop(0, heights // ROWS)
            def _(k):
                at = pl.ds(pl.multiple_of(k * ROWS, ROWS), ROWS)
                block = comb[c, :n1, :, at, :].reshape(n1 * bins * ROWS, radii)
                sums = dot(wides[x % 2][...], block).reshape(n2, bins, ROWS, radii)
                acc[c, :, at, :] = f_ref[:, s, x, at, :] + sums[0]
                for e in range(1, n2):
                    psend[c, e - 1, :, at, :] = sums[e].astype(jnp.bfloat16)

            for e in range(1, n2):
                partial_copy(s, x, e).start()

        @pl.when(s + ahead < species)
        def _():
            send_parents(s + ahead)

    def source(s):
        for x in range(cells):
            c = s * cells + x
            n2 = sizes(x)[1]
            for e in range(1, n2):
                partial_copy(s, x, e).wait_recv()

            @pl.loop(0, bins)
            def _(p):
                value = acc[c, p]
                for e in range(1, n2):
                    value = value + precv[c, e - 1, p].astype(jnp.float32)
                acc[c, p] = value
                rounded = value.astype(jnp.bfloat16)
                if x == 0:
                    faces_out[s, 0, p] = rounded
                if x == cells - 1:
                    faces_out[s, 1, p] = rounded

            if x == 0:
                face_copy(s, 0).start()
            if x == cells - 1:
                face_copy(s, 1).start()

    def diffuse(s):
        face_copy(s, 0).wait_recv()
        face_copy(s, 1).wait_recv()
        first = s * cells
        per = group // cells

        @pl.loop(0, bins // per)
        def _(k):
            planes = []
            for j in range(per):
                p = k * per + j
                own = [acc[first + x, p] for x in range(cells)]
                before = [faces_in[s, 1, p].astype(jnp.float32)] + own[:-1]
                after = own[1:] + [faces_in[s, 0, p].astype(jnp.float32)]
                for x in range(cells):
                    moved = coef[0] * own[x] + diff_ref[...] * (before[x] + after[x])
                    moved += coef[1] * pltpu.roll(own[x], 1, 1)
                    moved += coef[2] * pltpu.roll(own[x], radii - 1, 1)
                    planes.append(moved)
            moved = jnp.concatenate(planes, axis=0)
            high = moved.astype(jnp.bfloat16)
            low = (moved - high.astype(jnp.float32)).astype(jnp.bfloat16)
            settled = dot(height[0], high) + dot(height[0], low) + dot(height[1], high)
            for j in range(per):
                for x in range(cells):
                    n = j * cells + x
                    acc[first + x, k * per + j] = settled[n * heights : (n + 1) * heights]

        settled_copy(s).start()
        span = heights // 2
        for x in range(cells):
            @pl.loop(0, 2)
            def _(k):
                at = pl.ds(pl.multiple_of(k * span, span), span)
                carry = jnp.zeros((span, radii), jnp.float32)
                for p in range(bins - 1, -1, -1):
                    total = 2.0 * acc[first + x, p, at, :] + carry
                    carry = total - total * weight[p, x, at, :]
                below[s, x, at, :] = carry

    def relay(s):
        @pl.when(odd & (mom < count - 1))
        def _():
            h_copy(s, 0).wait_recv()

        @pl.when(mom % 2 == 0)
        def _():
            @pl.when(s == 0)
            def _():
                keep_above()

            below_copy(s).wait_recv()

            @pl.when(mom < count - 2)
            def _():
                h_copy(s, 1).wait_recv()

            for x in range(cells):
                entering = above[s, x] + keep[1, x] * hin[s, x]
                hin[s, x] = entering
                hout[s, x] = below[s, x] + keep[0, x] * entering

            @pl.when(mom > 0)
            def _():
                h_copy(s, 0).start()
                h_copy(s, 1).start()

    lag = (count - 1 - mom) // 2
    hold = 3

    @pl.loop(0, species + 3 + max(hold - 2, 0) + count // 2)
    def _(i):
        @pl.when(i < species)
        def _():
            mix(i)

        @pl.when((i >= 1) & (i < species + 1))
        def _():
            source(i - 1)

        @pl.when((i >= 2) & (i < species + 2))
        def _():
            diffuse(i - 2)

        for s in range(species):
            @pl.when(odd & (i == max(s + 2, hold)))
            def _():
                below_copy(s).start()

        s = i - 2 - max(hold - 2, 0) - lag

        @pl.when((s >= 0) & (s < species))
        def _():
            relay(s)

    @pl.when(odd)
    def _():
        rate_copy().wait_send()

    @pl.loop(0, species)
    def _(s):
        settled_copy(s).wait()
        for x in range(cells):
            for d in range(1, sizes(x)[0]):
                parent_copy(s, x, d).wait_send()
            for e in range(1, sizes(x)[1]):
                partial_copy(s, x, e).wait_send()
        face_copy(s, 0).wait_send()
        face_copy(s, 1).wait_send()

        @pl.when(odd)
        def _():
            below_copy(s).wait_send()

        @pl.when((mom % 2 == 0) & (mom > 0))
        def _():
            h_copy(s, 0).wait_send()
            h_copy(s, 1).wait_send()


def solve_kernel(settled_ref, hin_ref, weight_ref, out_ref):
    bins, _, heights, _ = weight_ref.shape
    span = heights // 2

    @pl.loop(0, 2)
    def _(k):
        at = pl.ds(pl.multiple_of(k * span, span), span)
        carry = hin_ref[0, 0, at, :]
        for p in range(bins - 1, -1, -1):
            settled = settled_ref[0, p, at, :]
            total = 2.0 * settled + carry
            both = total * weight_ref[p, 0, at, :]
            out_ref[p, 0, 0, at, :] = both - settled
            carry = total - both


def local(
    ny,
    nx,
    spectra,
    production,
    bin_group,
    parent_of,
    diffusivity,
    height_inverse,
    loss_rate,
    density,
):
    bins, species, cells, heights, radii = spectra.shape
    same = bin_group[:, None] == bin_group[None, :]
    kernel = jnp.where(same, production, jnp.zeros_like(production))
    chunks = species * cells
    block = (bins, heights, radii)
    plane = (heights, radii)
    most = max(nx, ny)
    group = cells * max(1, 256 // (heights * cells))
    dma = pltpu.SemaphoreType.DMA
    vmem = pl.BlockSpec(memory_space=pltpu.VMEM)
    hbm = pl.BlockSpec(memory_space=pltpu.HBM)
    free = pl.BlockSpec(memory_space=pl.ANY)
    stay = functools.partial(pltpu.with_memory_space_constraint, memory_space=pltpu.HBM)
    tall, broad = ny * bins * ROWS, nx * bins * ROWS
    settled, entering, weight = pl.pallas_call(
        functools.partial(step_kernel, ny, nx),
        out_shape=[
            jax.ShapeDtypeStruct((chunks,) + block, jnp.float32),
            jax.ShapeDtypeStruct((species, cells) + plane, jnp.float32),
            jax.ShapeDtypeStruct((bins, cells) + plane, jnp.float32),
        ],
        in_specs=[hbm, vmem, hbm, hbm, hbm, hbm, hbm],
        out_specs=[free, vmem, vmem],
        scratch_shapes=[
            pltpu.VMEM(spectra.shape, jnp.float32),
            pltpu.SMEM(parent_of.shape, jnp.int32),
            pltpu.VMEM(plane, jnp.float32),
            pltpu.VMEM(height_inverse.shape, jnp.float32),
            pltpu.SMEM(loss_rate.shape, jnp.float32),
            pltpu.VMEM(density.shape, jnp.float32),
            pltpu.VMEM((chunks, most) + block, jnp.bfloat16),
            pltpu.VMEM((chunks, most - 1) + block, jnp.bfloat16),
            pltpu.VMEM((chunks, most - 1) + block, jnp.bfloat16),
            pltpu.VMEM((chunks,) + block, jnp.float32),
            pltpu.VMEM((species, 2) + block, jnp.bfloat16),
            pltpu.VMEM((species, 2) + block, jnp.bfloat16),
            pltpu.VMEM((species, cells) + plane, jnp.float32),
            pltpu.VMEM((species, cells) + plane, jnp.float32),
            pltpu.VMEM((species, cells) + plane, jnp.float32),
            pltpu.VMEM((2, cells) + plane, jnp.float32),
            pltpu.VMEM((bins, 8, radii), jnp.float32),
            pltpu.VMEM((bins, 8, radii), jnp.float32),
            pltpu.VMEM((tall, broad), jnp.bfloat16),
            pltpu.VMEM((broad, tall), jnp.bfloat16),
            pltpu.VMEM((2, group * heights, group * heights), jnp.bfloat16),
            pltpu.VMEM((3,) + plane, jnp.float32),
            dma((6,)),
            dma((species,)),
            dma((chunks, most - 1)),
            dma((chunks, most - 1)),
            dma((chunks, most - 1)),
            dma((chunks, most - 1)),
            dma((species, 2)),
            dma((species, 2)),
            dma((species,)),
            dma((species,)),
            dma((species, 2)),
            dma((species,)),
            dma,
            dma,
        ],
        compiler_params=pltpu.CompilerParams(
            collective_id=0, has_side_effects=True, vmem_limit_bytes=28 * 1024 * 1024
        ),
    )(
        stay(spectra),
        kernel,
        stay(parent_of),
        stay(diffusivity),
        stay(height_inverse),
        stay(loss_rate),
        stay(density),
    )
    return pl.pallas_call(
        solve_kernel,
        grid=(cells, species),
        out_shape=jax.ShapeDtypeStruct(spectra.shape, jnp.float32),
        in_specs=[
            pl.BlockSpec((1,) + block, lambda x, s: (s * cells + x, 0, 0, 0)),
            pl.BlockSpec((1, 1) + plane, lambda x, s: (s, x, 0, 0)),
            pl.BlockSpec((bins, 1) + plane, lambda x, s: (0, x, 0, 0)),
        ],
        out_specs=pl.BlockSpec((bins, 1, 1) + plane, lambda x, s: (0, s, x, 0, 0)),
        compiler_params=pltpu.CompilerParams(vmem_limit_bytes=16 * 1024 * 1024),
    )(settled, entering, weight)


def solution(mesh):
    ny, nx = grid_of(mesh.shape["mom"])
    return jax.shard_map(
        functools.partial(local, ny, nx),
        mesh=mesh,
        in_specs=(
            P("mom", None, "phi", None, None),
            P(),
            P(),
            P(),
            P(),
            P(),
            P("mom"),
            P("phi", None, None),
        ),
        out_specs=P("mom", None, "phi", None, None),
        check_vma=False,
    )
```

profile of v0, /device:TPU:1, one launch (start us, length us, event | category | flops | bytes accessed | tf_op | source)
XLA Modules:
  0.0 78.2 jit_solution(5816536212041962650)
XLA Ops:
  0.0 0.8 %compare_select_fusion.kernel_ref = bf16[32,32]{1,0:T(8,128)(2,1)S(1)} fusion(bf16[32,32]{1,0:T(8,128)(2,1)} %param.9, s32[32]{0:T(128)} %param.10), kind=kLoop, calls=%fused_computation | loop fusion | flops 2048 | bytes 4224 | tf_op jit(solution)/shard_map/jit(_where)/select_n | solution.py:489
  0.8 73.5 %shard_map.82 = (f32[8,8,64,256]{3,2,1,0:T(8,128)S(1)}, f32[4,2,64,256]{3,2,1,0:T(8,128)S(1)}, f32[8,2,64,256]{3,2,1,0:T(8,128)S(1)}) custom-call(f32[8,4,2,64,256]{4,3,2,1,0:T(8,128)} %f_hbm.1, bf16[32,32]{1,0:T(8,128)(2,1)S(1)} %compare_select_fusion.kernel_ref, s32[4]{0:T(128)} %parent_hbm.1, f32[64,256]{1,0:T(8,128)} %diff_hbm.1, f32[64,64]{1,0:T(8,128)} %inverse_hbm.1, ...), custom_call_target="tpu_custom_call" | custom-call | tf_op jit(solution)/shard_map/pallas_call | solution.py:501
  74.4 3.9 %shard_map.83 = f32[8,4,2,64,256]{4,3,2,1,0:T(8,128)} custom-call(f32[8,8,64,256]{3,2,1,0:T(8,128)S(1)} %get-tuple-element.8.settled_ref, f32[4,2,64,256]{3,2,1,0:T(8,128)S(1)} %get-tuple-element.9.hin_ref, f32[8,2,64,256]{3,2,1,0:T(8,128)S(1)} %get-tuple-element.10.weight_ref), custom_call_target="tpu_custom_call" | custom-call | tf_op jit(solution)/shard_map/pallas_call | solution.py:560
where the time goes:
time: 78.4 us; the launch traced here: 78.2 us
  Pallas kernels  77.4 us (99%)
  other arithmetic  0.8 us (1%)
    pallas_call x1, Pallas kernels, local(): pl.pallas_call(functools.partial(step_kernel, ny, nx), out_shape=[jax.Sha...  73.5 us
    pallas_call x1, Pallas kernels, local(): pl.pallas_call(solve_kernel, grid=(cells, species), out_shape=jax.ShapeDt...  3.88 us

commit v1 on v0

v1 whole, which is shorter than its diff:
```python
import functools
import math

import jax
import jax.numpy as jnp
from jax import lax
from jax.experimental import pallas as pl
from jax.experimental.pallas import tpu as pltpu
from jax.sharding import PartitionSpec as P

MESH = pl.DeviceIdType.MESH
ROWS = 16


def grid_of(count):
    columns = max(d for d in range(1, math.isqrt(count) + 1) if count % d == 0)
    return count // columns, columns


def dot(a, b):
    return jnp.dot(a, b, preferred_element_type=jnp.float32)


def dot_nt(a, b):
    return lax.dot_general(a, b, (((1,), (1,)), ((), ())), preferred_element_type=jnp.float32)


def onehot_bins(first_bins, bins, total):
    local = lax.broadcasted_iota(jnp.int32, (bins, ROWS, total), 0)
    whole = lax.broadcasted_iota(jnp.int32, (bins, ROWS, total), 2)
    parts = [
        jnp.where(local + first == whole, 1.0, 0.0).reshape(bins * ROWS, total)
        for first in first_bins
    ]
    return jnp.concatenate(parts, axis=0).astype(jnp.bfloat16)


def classes(parent_ref):
    n = parent_ref.shape[0]
    parent = [parent_ref[s] for s in range(n)]
    keys = []
    for s in range(n):
        size, first = 0, n
        for j in range(n - 1, -1, -1):
            equal = parent[j] == parent[s]
            size = size + jnp.where(equal, 1, 0)
            first = jnp.where(equal, j, first)
        keys.append((n - size) * (n * n) + first * n + s)
    ranks = [sum(jnp.where(keys[j] < keys[s], 1, 0) for j in range(n) if j != s) for s in range(n)]
    return [sum(jnp.where(ranks[s] == i, s, 0) for s in range(1, n)) for i in range(n)]


def step_kernel(
    ny,
    nx,
    kids,
    f_hbm,
    production_hbm,
    group_hbm,
    parent_hbm,
    diff_hbm,
    inverse_hbm,
    rate_hbm,
    density_hbm,
    acc,
    hin,
    weight,
    f_parts,
    parent_ref,
    group_ref,
    production_ref,
    diff_ref,
    inverse_ref,
    rate_ref,
    density_ref,
    comb,
    psend,
    precv,
    own_part,
    faces_out,
    faces_in,
    below,
    above,
    hout,
    keep,
    rates_out,
    rates_in,
    wide_0,
    wide_1,
    height,
    coef,
    in_sem,
    f_sem,
    x_send,
    x_recv,
    y_send,
    y_recv,
    f_send,
    f_recv,
    a_send,
    a_recv,
    h_send,
    h_recv,
    r_send,
    r_recv,
):
    bins, species, cells, _, radii = f_parts[0].shape
    heights = diff_ref.shape[0]
    pieces = len(f_parts)
    total_bins = production_ref.shape[0]
    count = ny * nx
    slots = len(kids)
    starts = [sum(kids[:t]) for t in range(slots)]
    wides = (wide_0, wide_1)
    phi = lax.axis_index("phi")
    mom = lax.axis_index("mom")
    phis = lax.axis_size("phi")
    row, col = mom // nx, mom % nx
    right, left = (phi + 1) % phis, (phi + phis - 1) % phis

    small = [
        pltpu.make_async_copy(parent_hbm, parent_ref, in_sem.at[0]),
        pltpu.make_async_copy(group_hbm, group_ref, in_sem.at[1]),
        pltpu.make_async_copy(production_hbm, production_ref, in_sem.at[2]),
        pltpu.make_async_copy(rate_hbm, rate_ref, in_sem.at[3]),
        pltpu.make_async_copy(diff_hbm, diff_ref, in_sem.at[4]),
        pltpu.make_async_copy(inverse_hbm, inverse_ref, in_sem.at[5]),
        pltpu.make_async_copy(density_hbm, density_ref, in_sem.at[6]),
    ]
    loads = [
        pltpu.make_async_copy(f_hbm.at[:, :, :, pl.ds(k * ROWS, ROWS), :], f_parts[k], f_sem.at[k])
        for k in range(pieces)
    ]
    small[0].start()
    for copy in loads:
        copy.start()
    for copy in small[1:]:
        copy.start()
    barrier = pltpu.get_barrier_semaphore()
    for d in range(1, count):
        pl.semaphore_signal(
            barrier, inc=1, device_id={"mom": (mom + d) % count}, device_id_type=MESH
        )
    for side in (left, right):
        pl.semaphore_signal(barrier, inc=1, device_id={"phi": side}, device_id_type=MESH)

    def along_row(d):
        return {"mom": row * nx + (col + d) % nx}

    def along_col(e):
        return {"mom": ((row + e) % ny) * nx + col}

    def sizes(x):
        return (nx, ny) if x % 2 == 0 else (ny, nx)

    def parent_copy(t, x, d, k):
        c = t * cells + x
        return pltpu.make_async_remote_copy(
            src_ref=comb.at[c, 0, k],
            dst_ref=comb.at[c, d, k],
            send_sem=x_send.at[c, d - 1, k],
            recv_sem=x_recv.at[c, d - 1, k],
            device_id=along_row(d) if x % 2 == 0 else along_col(d),
            device_id_type=MESH,
        )

    def partial_copy(t, x, e, k):
        c = t * cells + x
        return pltpu.make_async_remote_copy(
            src_ref=psend.at[c, e - 1, k],
            dst_ref=precv.at[c, e - 1, k],
            send_sem=y_send.at[c, e - 1, k],
            recv_sem=y_recv.at[c, e - 1, k],
            device_id=along_col(e) if x % 2 == 0 else along_row(e),
            device_id_type=MESH,
        )

    def face_copy(i, side, k):
        return pltpu.make_async_remote_copy(
            src_ref=faces_out.at[i, side, k],
            dst_ref=faces_in.at[i, side, k],
            send_sem=f_send.at[i, side, k],
            recv_sem=f_recv.at[i, side, k],
            device_id={"phi": left if side == 0 else right},
            device_id_type=MESH,
        )

    def below_copy(i, x):
        return pltpu.make_async_remote_copy(
            src_ref=below.at[i, x],
            dst_ref=above.at[i, x],
            send_sem=a_send.at[i, x],
            recv_sem=a_recv.at[i, x],
            device_id={"mom": (mom + count - 1) % count},
            device_id_type=MESH,
        )

    def h_copy(i, x, n):
        return pltpu.make_async_remote_copy(
            src_ref=hout.at[i, x],
            dst_ref=hin.at[i, x],
            send_sem=h_send.at[i, x, n],
            recv_sem=h_recv.at[i, x],
            device_id={"mom": (mom + count - 1 - n) % count},
            device_id_type=MESH,
        )

    def rate_copy():
        return pltpu.make_async_remote_copy(
            src_ref=rates_out,
            dst_ref=rates_in,
            send_sem=r_send,
            recv_sem=r_recv,
            device_id={"mom": (mom + count - 1) % count},
            device_id_type=MESH,
        )

    def fill_parents(t, k):
        parent = parent_ref[order[starts[t]]]
        for x in range(cells):
            comb[t * cells + x, 0, k] = f_parts[k][:, parent, x].astype(jnp.bfloat16)

    def send_parents(t, k):
        for x in range(cells):
            for d in range(1, sizes(x)[0]):
                parent_copy(t, x, d, k).start()

    odd = mom % 2 == 1
    ahead = 2
    small[0].wait()
    order = classes(parent_ref)
    for k in range(pieces):
        loads[k].wait()
        fill_parents(0, k)
        if k == 0:
            pl.semaphore_wait(barrier, count + 1)
        send_parents(0, k)
    for t in range(1, slots):
        for k in range(pieces):
            fill_parents(t, k)
            if t < ahead:
                send_parents(t, k)

    for copy in small[1:]:
        copy.wait()
    for p in range(bins):
        rates_out[pl.ds(p, 1), :] = jnp.full((1, radii), rate_ref[p], jnp.float32)

    @pl.when(odd)
    def _():
        rate_copy().start()

    p_at = lax.broadcasted_iota(jnp.int32, (total_bins, total_bins), 0)
    q_at = lax.broadcasted_iota(jnp.int32, (total_bins, total_bins), 1)
    p_group = jnp.zeros((total_bins, total_bins), jnp.int32)
    q_group = jnp.zeros((total_bins, total_bins), jnp.int32)
    for b in range(total_bins):
        p_group = jnp.where(p_at == b, group_ref[b], p_group)
        q_group = jnp.where(q_at == b, group_ref[b], q_group)
    kernel = jnp.where(p_group == q_group, production_ref[...].astype(jnp.float32), 0.0)
    kernel = kernel.astype(jnp.bfloat16)
    row_starts = [(row * nx + (col + d) % nx) * bins for d in range(nx)]
    col_starts = [(((row + e) % ny) * nx + col) * bins for e in range(ny)]
    row_froms = [(row * nx + (col + nx - d) % nx) * bins for d in range(nx)]
    col_froms = [(((row + ny - e) % ny) * nx + col) * bins for e in range(ny)]
    for to, source_from, ref in ((col_starts, row_froms, wide_0), (row_starts, col_froms, wide_1)):
        rows_1h = onehot_bins(to, bins, total_bins)
        cols_1h = onehot_bins(source_from, bins, total_bins)
        mixed = dot_nt(dot(rows_1h, kernel).astype(jnp.bfloat16), cols_1h)
        r_at = lax.broadcasted_iota(jnp.int32, mixed.shape, 0) & (ROWS - 1)
        c_at = lax.broadcasted_iota(jnp.int32, mixed.shape, 1) & (ROWS - 1)
        ref[...] = jnp.where(r_at == c_at, mixed, 0.0).astype(jnp.bfloat16)

    group = height.shape[1] // heights
    a_at = lax.broadcasted_iota(jnp.int32, (heights, heights), 0)
    b_at = lax.broadcasted_iota(jnp.int32, (heights, heights), 1)
    stencil = jnp.where(a_at == b_at, 0.5, 0.0) + jnp.where(jnp.abs(a_at - b_at) == 1, 0.25, 0.0)
    both = jnp.dot(
        inverse_ref[...],
        stencil,
        precision=lax.Precision.HIGHEST,
        preferred_element_type=jnp.float32,
    )
    high = both.astype(jnp.bfloat16).astype(jnp.float32)
    tall_a = lax.broadcasted_iota(jnp.int32, (group, heights, heights), 1)
    tall_b = lax.broadcasted_iota(jnp.int32, (group, heights, heights), 2)
    spread = jnp.where(tall_a == tall_b, 1.0, 0.0).reshape(group * heights, heights)
    spread = spread.astype(jnp.bfloat16)
    row_g = lax.broadcasted_iota(jnp.int32, (group, heights, group * heights), 0)
    col_g = lax.broadcasted_iota(jnp.int32, (group, heights, group * heights), 2)
    first = row_g * heights
    inside = jnp.where((col_g >= first) & (col_g < first + heights), 1.0, 0.0)
    inside = inside.reshape(group * heights, group * heights)
    for n, part in enumerate((high, both - high)):
        tall = jnp.concatenate([part] * group, axis=0).astype(jnp.bfloat16)
        height[n] = (dot_nt(tall, spread) * inside).astype(jnp.bfloat16)

    diff = diff_ref[...]
    lane = lax.broadcasted_iota(jnp.int32, diff.shape, 1)
    coef[0] = 1.0 - 3.0 * diff
    coef[1] = jnp.where(lane == 0, 0.0, 0.5 * diff)
    coef[2] = jnp.where(lane == radii - 1, 0.0, 0.5 * diff)

    for x in range(cells):
        kept = jnp.ones((heights, radii), jnp.float32)
        for p in range(bins):
            part = 1.0 / (1.0 + 0.5 * rate_ref[p] * density_ref[x])
            weight[p, x] = part
            kept = kept * (1.0 - part)
        keep[0, x] = kept

    def keep_above():
        rate_copy().wait_recv()
        for x in range(cells):
            kept = jnp.ones((heights, radii), jnp.float32)
            for p in range(bins):
                kept = kept * (1.0 - 1.0 / (1.0 + 0.5 * rates_in[pl.ds(p, 1), :] * density_ref[x]))
            keep[1, x] = kept

    @pl.when(mom >= count - 2)
    def _():
        hin[...] = jnp.zeros_like(hin)

    def mix(t):
        for k in range(pieces):
            for x in range(cells):
                c = t * cells + x
                n1, n2 = sizes(x)
                for d in range(1, n1):
                    parent_copy(t, x, d, k).wait_recv()
                block = comb[c, :n1, k].reshape(n1 * bins * ROWS, radii)
                sums = dot(wides[x % 2][...], block).reshape(n2, bins, ROWS, radii)
                own_part[c, k] = sums[0]
                for e in range(1, n2):
                    psend[c, e - 1, k] = sums[e].astype(jnp.bfloat16)
                    partial_copy(t, x, e, k).start()
        if t + ahead < slots:
            for k in range(pieces):
                send_parents(t + ahead, k)

    def source(t):
        for k in range(pieces):
            at = pl.ds(k * ROWS, ROWS)
            for x in range(cells):
                c = t * cells + x
                n2 = sizes(x)[1]
                for e in range(1, n2):
                    partial_copy(t, x, e, k).wait_recv()

                @pl.loop(0, bins)
                def _(p):
                    value = own_part[c, k, p]
                    for e in range(1, n2):
                        value = value + precv[c, e - 1, k, p].astype(jnp.float32)
                    for i in range(starts[t], starts[t] + kids[t]):
                        total = f_parts[k][p, order[i], x] + value
                        acc[i * cells + x, p, at, :] = total
                        rounded = total.astype(jnp.bfloat16)
                        if x == 0:
                            faces_out[i, 0, k, p] = rounded
                        if x == cells - 1:
                            faces_out[i, 1, k, p] = rounded

                for i in range(starts[t], starts[t] + kids[t]):
                    if x == 0:
                        face_copy(i, 0, k).start()
                    if x == cells - 1:
                        face_copy(i, 1, k).start()

    def diffuse(i):
        for k in range(pieces):
            face_copy(i, 0, k).wait_recv()
            face_copy(i, 1, k).wait_recv()
        first = i * cells
        per = group // cells

        @pl.loop(0, bins // per)
        def _(k):
            planes = []
            for j in range(per):
                p = k * per + j
                own = [acc[first + x, p] for x in range(cells)]
                ends = [
                    faces_in[i, side, :, p].reshape(heights, radii).astype(jnp.float32)
                    for side in range(2)
                ]
                before = [ends[1]] + own[:-1]
                after = own[1:] + [ends[0]]
                for x in range(cells):
                    moved = coef[0] * own[x] + diff_ref[...] * (before[x] + after[x])
                    moved += coef[1] * pltpu.roll(own[x], 1, 1)
                    moved += coef[2] * pltpu.roll(own[x], radii - 1, 1)
                    planes.append(moved)
            moved = jnp.concatenate(planes, axis=0)
            high = moved.astype(jnp.bfloat16)
            low = (moved - high.astype(jnp.float32)).astype(jnp.bfloat16)
            settled = dot(height[0], high) + dot(height[0], low) + dot(height[1], high)
            for j in range(per):
                for x in range(cells):
                    n = j * cells + x
                    acc[first + x, k * per + j] = settled[n * heights : (n + 1) * heights]

        span = heights // 2
        for x in range(cells):
            @pl.loop(0, 2)
            def _(k):
                at = pl.ds(pl.multiple_of(k * span, span), span)
                carry = jnp.zeros((span, radii), jnp.float32)
                for p in range(bins - 1, -1, -1):
                    total = 2.0 * acc[first + x, p, at, :] + carry
                    carry = total - total * weight[p, x, at, :]
                below[i, x, at, :] = carry

    def send_below(i):
        @pl.when(odd)
        def _():
            for x in range(cells):
                below_copy(i, x).start()

    def diffuse_slot(t, send):
        @pl.loop(starts[t], starts[t] + kids[t])
        def _(i):
            diffuse(i)
            if send:
                send_below(i)

    def relay(i):
        for x in range(cells):
            below_copy(i, x).wait_recv()

            @pl.when(mom < count - 2)
            def _():
                h_copy(i, x, 1).wait_recv()

            entering = above[i, x] + keep[1, x] * hin[i, x]
            hin[i, x] = entering
            hout[i, x] = below[i, x] + keep[0, x] * entering

            @pl.when(mom > 0)
            def _():
                h_copy(i, x, 0).start()
                h_copy(i, x, 1).start()

    lag = (count - 1 - mom) // 2
    early = species - kids[-1]
    for i in range(slots + 1):
        if i < slots:
            mix(i)
        if 1 <= i:
            source(i - 1)
        if i >= 2:
            diffuse_slot(i - 2, False)
        if i == max(slots - 1, 0):
            @pl.when(mom % 2 == 0)
            def _():
                keep_above()

        if i == slots - 1:
            @pl.loop(0, sum(kids[: max(slots - 2, 0)]))
            def _(i):
                send_below(i)
        if i == slots:
            @pl.loop(sum(kids[: max(slots - 2, 0)]), early)
            def _(i):
                send_below(i)

    @pl.when((mom % 2 == 0) & (lag == 0))
    def _():
        @pl.loop(0, early)
        def _(i):
            relay(i)

    diffuse_slot(slots - 1, True)

    @pl.when((mom % 2 == 0) & (lag > 0))
    def _():
        @pl.loop(0, early)
        def _(i):
            relay(i)

    @pl.when(mom % 2 == 0)
    def _():
        @pl.loop(early, species)
        def _(i):
            relay(i)

    @pl.when(odd)
    def _():
        rate_copy().wait_send()

    for t in range(slots):
        for k in range(pieces):
            for x in range(cells):
                for d in range(1, sizes(x)[0]):
                    parent_copy(t, x, d, k).wait_send()
                for e in range(1, sizes(x)[1]):
                    partial_copy(t, x, e, k).wait_send()

    @pl.loop(0, species)
    def _(i):
        for k in range(pieces):
            face_copy(i, 0, k).wait_send()
            face_copy(i, 1, k).wait_send()
        for x in range(cells):
            @pl.when(odd)
            def _():
                below_copy(i, x).wait_send()

            @pl.when(odd & (mom < count - 1))
            def _():
                h_copy(i, x, 0).wait_recv()

            @pl.when((mom % 2 == 0) & (mom > 0))
            def _():
                h_copy(i, x, 0).wait_send()
                h_copy(i, x, 1).wait_send()


def solve_kernel(
    settled_ref, hin_ref, weight_ref, parent_hbm, out_hbm, done, parent_ref, in_sem, out_sem
):
    bins, cells, heights, radii = weight_ref.shape
    species = parent_ref.shape[0]
    span = heights // 2
    load = pltpu.make_async_copy(parent_hbm, parent_ref, in_sem)
    load.start()
    order = None
    copies = []
    for i in range(species):
        for x in range(cells):
            n = i * cells + x

            @pl.loop(0, 2)
            def _(k):
                at = pl.ds(pl.multiple_of(k * span, span), span)
                carry = hin_ref[i, x, at, :]
                for p in range(bins - 1, -1, -1):
                    settled = settled_ref[n, p, at, :]
                    total = 2.0 * settled + carry
                    both = total * weight_ref[p, x, at, :]
                    done[n, p, at, :] = both - settled
                    carry = total - both

            if order is None:
                load.wait()
                order = classes(parent_ref)
            copy = pltpu.make_async_copy(done.at[n], out_hbm.at[:, order[i], x], out_sem.at[n])
            copy.start()
            copies.append(copy)
    for copy in copies:
        copy.wait()


def local(
    ny,
    nx,
    which,
    kids,
    spectra,
    production,
    bin_group,
    parent_of,
    diffusivity,
    height_inverse,
    loss_rate,
    density,
):
    bins, species, cells, heights, radii = spectra.shape
    chunks = len(kids) * cells
    block = (bins, heights, radii)
    plane = (heights, radii)
    pieces = heights // ROWS
    split = (pieces, bins, ROWS, radii)
    most = max(nx, ny)
    group = cells * max(1, 256 // (heights * cells))
    dma = pltpu.SemaphoreType.DMA
    vmem = pl.BlockSpec(memory_space=pltpu.VMEM)
    hbm = pl.BlockSpec(memory_space=pltpu.HBM)
    stay = functools.partial(pltpu.with_memory_space_constraint, memory_space=pltpu.HBM)
    tall, broad = ny * bins * ROWS, nx * bins * ROWS
    settled, entering, weight = pl.pallas_call(
        functools.partial(step_kernel, ny, nx, kids),
        out_shape=[
            jax.ShapeDtypeStruct((species * cells,) + block, jnp.float32),
            jax.ShapeDtypeStruct((species, cells) + plane, jnp.float32),
            jax.ShapeDtypeStruct((bins, cells) + plane, jnp.float32),
        ],
        in_specs=[hbm] * 8,
        out_specs=[vmem, vmem, vmem],
        scratch_shapes=[
            [pltpu.VMEM((bins, species, cells, ROWS, radii), jnp.float32) for _ in range(pieces)],
            pltpu.SMEM(parent_of.shape, jnp.int32),
            pltpu.SMEM(bin_group.shape, jnp.int32),
            pltpu.VMEM(production.shape, jnp.bfloat16),
            pltpu.VMEM(plane, jnp.float32),
            pltpu.VMEM(height_inverse.shape, jnp.float32),
            pltpu.SMEM(loss_rate.shape, jnp.float32),
            pltpu.VMEM(density.shape, jnp.float32),
            pltpu.VMEM((chunks, most) + split, jnp.bfloat16),
            pltpu.VMEM((chunks, most - 1) + split, jnp.bfloat16),
            pltpu.VMEM((chunks, most - 1) + split, jnp.bfloat16),
            pltpu.VMEM((chunks,) + split, jnp.float32),
            pltpu.VMEM((species, 2) + split, jnp.bfloat16),
            pltpu.VMEM((species, 2) + split, jnp.bfloat16),
            pltpu.VMEM((species, cells) + plane, jnp.float32),
            pltpu.VMEM((species, cells) + plane, jnp.float32),
            pltpu.VMEM((species, cells) + plane, jnp.float32),
            pltpu.VMEM((2, cells) + plane, jnp.float32),
            pltpu.VMEM((max(bins, 8), radii), jnp.float32),
            pltpu.VMEM((max(bins, 8), radii), jnp.float32),
            pltpu.VMEM((tall, broad), jnp.bfloat16),
            pltpu.VMEM((broad, tall), jnp.bfloat16),
            pltpu.VMEM((2, group * heights, group * heights), jnp.bfloat16),
            pltpu.VMEM((3,) + plane, jnp.float32),
            dma((7,)),
            dma((pieces,)),
            dma((chunks, most - 1, pieces)),
            dma((chunks, most - 1, pieces)),
            dma((chunks, most - 1, pieces)),
            dma((chunks, most - 1, pieces)),
            dma((species, 2, pieces)),
            dma((species, 2, pieces)),
            dma((species, cells)),
            dma((species, cells)),
            dma((species, cells, 2)),
            dma((species, cells)),
            dma,
            dma,
        ],
        compiler_params=pltpu.CompilerParams(
            collective_id=which, has_side_effects=True, vmem_limit_bytes=40 * 1024 * 1024
        ),
    )(*(stay(a) for a in (
        spectra, production, bin_group, parent_of, diffusivity, height_inverse, loss_rate, density
    )))
    return pl.pallas_call(
        solve_kernel,
        out_shape=jax.ShapeDtypeStruct(spectra.shape, jnp.float32),
        in_specs=[vmem, vmem, vmem, hbm],
        out_specs=hbm,
        scratch_shapes=[
            pltpu.VMEM((species * cells,) + block, jnp.float32),
            pltpu.SMEM(parent_of.shape, jnp.int32),
            dma,
            dma((species * cells,)),
        ],
        compiler_params=pltpu.CompilerParams(vmem_limit_bytes=16 * 1024 * 1024),
    )(settled, entering, weight, stay(parent_of))


def step(ny, nx, *args):
    parent_of = args[3]
    species = parent_of.shape[0]
    single = (1,) * species
    if species != 4:
        return local(ny, nx, 0, single, *args)
    pairs = jnp.sum((parent_of[:, None] == parent_of[None, :]).astype(jnp.int32))
    which = jnp.where(pairs > 8, 0, jnp.where(pairs > 6, 1, jnp.where(pairs > 4, 2, 3)))
    forms = ((3, 1), (2, 2), (2, 1, 1), single)
    return lax.switch(
        which, [functools.partial(local, ny, nx, n, kids) for n, kids in enumerate(forms)], *args
    )


def solution(mesh):
    ny, nx = grid_of(mesh.shape["mom"])
    return jax.shard_map(
        functools.partial(step, ny, nx),
        mesh=mesh,
        in_specs=(
            P("mom", None, "phi", None, None),
            P(),
            P(),
            P(),
            P(),
            P(),
            P("mom"),
            P("phi", None, None),
        ),
        out_specs=P("mom", None, "phi", None, None),
        check_vma=False,
    )
```

time: 78.4 us -> 63.9 us (0.82)
  Pallas kernels: 77.4 us -> 58.4 us
  local copies, waits for them, and re-layouts: 0 us -> 2.01 us
  between operations: 0.01 us -> 1.97 us
    pallas_call x2, Pallas kernels: 77.4 us -> 58.4 us  [the longest x1 56.6 us: local(): pl.pallas_call(functools.partial(step_kernel, ny, nx, kids), out_shape=[j...]
    unnamed x0 -> x2, local copies, waits for them, and re-layouts: none -> 2.01 us
    reduce_sum x0 -> x1, other arithmetic: none -> 1.43 us  [step(): jnp.sum((parent_of[:, None] == parent_of[None, :]).astype(jnp.int32))]
    select_n x1 -> x0, other arithmetic: 0.8 us -> none  [local(): kernel = jnp.where(same, production, jnp.zeros_like(production))]
where the time goes in v1:
time: 63.9 us; the launch traced here: 64.4 us
  Pallas kernels  58.4 us (91%)
  local copies, waits for them, and re-layouts  2.01 us (3%)
  between operations  1.97 us (3%)
  other arithmetic  1.43 us (2%)
    pallas_call x1, Pallas kernels, local(): pl.pallas_call(functools.partial(step_kernel, ny, nx, kids), out_shape=[j...  56.6 us
    unnamed x2, local copies, waits for them, and re-layouts  2.01 us
    pallas_call x1, Pallas kernels, local(): pl.pallas_call(solve_kernel, out_shape=jax.ShapeDtypeStruct(spectra.shape...  1.81 us
    reduce_sum x1, other arithmetic, step(): jnp.sum((parent_of[:, None] == parent_of[None, :]).astype(jnp.int32))  1.43 us

profile of v1, /device:TPU:1, one launch (start us, length us, event | category | flops | bytes accessed | tf_op | source)
XLA Modules:
  0.0 64.4 jit_solution(10978426878453318053)
XLA Ops:
  0.0 1.4 %convert_reduce_fusion = s32[]{:T(128)} fusion(s32[4]{0:T(128)} %param.15), kind=kLoop, calls=%fused_computation | loop fusion | flops 47 | bytes 20 | tf_op jit(solution)/shard_map/reduce_sum | solution.py:657
  3.4 59.0 %conditional.1 = (f32[8,4,2,64,256]{4,3,2,1,0:T(8,128)S(1)}) conditional(s32[]{:T(128)} %clamp.3, (f32[8,4,2,64,256]{4,3,2,1,0:T(8,128)}, bf16[32,32]{1,0:T(8,128)(2,1)}, s32[32]{0:T(128)}, s32[4]{0:T(128)}, f32[64,256]{1,0:T(8,128)}, /*index=5*/f32[64,64]{1,0:T(8,128)}, f32[8]{0:T(128)}, ...), branch_computations={%region_1.2_spmd, %region_2.3_spmd, %region_3.4_spmd, %region_4.5_... | conditional | bytes 8 | solution.py:660
  3.4 56.6 %branch_2_fun.2 = (f32[8,8,64,256]{3,2,1,0:T(8,128)S(1)}, f32[4,2,64,256]{3,2,1,0:T(8,128)S(1)}, f32[8,2,64,256]{3,2,1,0:T(8,128)S(1)}) custom-call(f32[8,4,2,64,256]{4,3,2,1,0:T(8,128)} %get-tuple-element.96.f_hbm, bf16[32,32]{1,0:T(8,128)(2,1)} %get-tuple-element.97.production_hbm, s32[32]{0:T(128)} %get-tuple-element.98.group_hbm, ...), custom_call_target="tpu_custom_call" | custom-call | tf_op jit(solution)/shard_map/cond/branch_2_fun/pallas_call | solution.py:581
  60.1 1.8 %branch_2_fun.3 = f32[8,4,2,64,256]{4,3,2,1,0:T(8,128)S(1)} custom-call(f32[8,8,64,256]{3,2,1,0:T(8,128)S(1)} %get-tuple-element.104.settled_ref, f32[4,2,64,256]{3,2,1,0:T(8,128)S(1)} %get-tuple-element.105.hin_ref, f32[8,2,64,256]{3,2,1,0:T(8,128)S(1)} %get-tuple-element.106.weight_ref, s32[4]{0:T(128)} %get-tuple-element.99.parent_hbm), custom_call_target="tpu_custom_call" | custom-call | tf_op jit(solution)/shard_map/cond/branch_2_fun/pallas_call | solution.py:636
  62.4 0.0 copy-start
  62.4 2.0 %copy-done = f32[8,4,2,64,256]{4,3,2,1,0:T(8,128)} copy-done((f32[8,4,2,64,256]{4,3,2,1,0:T(8,128)}, f32[8,4,2,64,256]{4,3,2,1,0:T(8,128)S(1)}, u32[]{:S(2)}) %copy-start) | copy-done | bytes 4194328
Async XLA Ops:
  62.4 2.0 %copy-start = (f32[8,4,2,64,256]{4,3,2,1,0:T(8,128)}, f32[8,4,2,64,256]{4,3,2,1,0:T(8,128)S(1)}, u32[]{:S(2)}) copy-start(f32[8,4,2,64,256]{4,3,2,1,0:T(8,128)S(1)} %get-tuple-element.123) | copy-start | bytes 12582916

commit v2 on v1

--- a/solution.py
+++ b/solution.py
@@ -3,6 +3,7 @@
 
 import jax
 import jax.numpy as jnp
+import numpy as np
 from jax import lax
 from jax.experimental import pallas as pl
 from jax.experimental.pallas import tpu as pltpu
@@ -10,6 +11,9 @@
 
 MESH = pl.DeviceIdType.MESH
 ROWS = 16
+VMEM = pl.BlockSpec(memory_space=pltpu.VMEM)
+HBM = pl.BlockSpec(memory_space=pltpu.HBM)
+stay = functools.partial(pltpu.with_memory_space_constraint, memory_space=pltpu.HBM)
 
 
 def grid_of(count):
@@ -33,6 +37,17 @@
         for first in first_bins
     ]
     return jnp.concatenate(parts, axis=0).astype(jnp.bfloat16)
+
+
+def coded(value):
+    fourth = (value * value) * (value * value)
+    return jnp.where(value < 0.0, -fourth, fourth).astype(jnp.bfloat16)
+
+
+def decoded(code):
+    code = code.astype(jnp.float32)
+    root = jnp.sqrt(jnp.sqrt(jnp.abs(code)))
+    return jnp.where(code < 0.0, -root, root)
 
 
 def classes(parent_ref):
@@ -63,10 +78,9 @@
     rate_hbm,
     density_hbm,
     acc,
-    hin,
-    weight,
-    f_parts,
+    f_ref,
     parent_ref,
+    order_ref,
     group_ref,
     production_ref,
     diff_ref,
@@ -80,8 +94,12 @@
     faces_out,
     faces_in,
     below,
+    below_out,
     above,
+    entered,
+    hin,
     hout,
+    weight,
     keep,
     rates_out,
     rates_in,
@@ -104,19 +122,23 @@
     r_send,
     r_recv,
 ):
-    bins, species, cells, _, radii = f_parts[0].shape
-    heights = diff_ref.shape[0]
-    pieces = len(f_parts)
+    bins, species, cells, heights, radii = f_ref.shape
+    pieces = heights // ROWS
     total_bins = production_ref.shape[0]
     count = ny * nx
     slots = len(kids)
-    starts = [sum(kids[:t]) for t in range(slots)]
     wides = (wide_0, wide_1)
     phi = lax.axis_index("phi")
     mom = lax.axis_index("mom")
     phis = lax.axis_size("phi")
     row, col = mom // nx, mom % nx
     right, left = (phi + 1) % phis, (phi + phis - 1) % phis
+
+    def first_of(t):
+        return sum(jnp.where(t > j, kids[j], 0) for j in range(slots))
+
+    def rows(k):
+        return pl.ds(pl.multiple_of(k * ROWS, ROWS), ROWS)
 
     small = [
         pltpu.make_async_copy(parent_hbm, parent_ref, in_sem.at[0]),
@@ -128,7 +150,11 @@
         pltpu.make_async_copy(density_hbm, density_ref, in_sem.at[6]),
     ]
     loads = [
-        pltpu.make_async_copy(f_hbm.at[:, :, :, pl.ds(k * ROWS, ROWS), :], f_parts[k], f_sem.at[k])
+        pltpu.make_async_copy(
+            f_hbm.at[:, :, :, pl.ds(k * ROWS, ROWS), :],
+            f_ref.at[:, :, :, pl.ds(k * ROWS, ROWS), :],
+            f_sem.at[k],
+        )
         for k in range(pieces)
     ]
     small[0].start()
@@ -187,7 +213,7 @@
 
     def below_copy(i, x):
         return pltpu.make_async_remote_copy(
-            src_ref=below.at[i, x],
+            src_ref=below_out.at[i, x],
             dst_ref=above.at[i, x],
             send_sem=a_send.at[i, x],
             recv_sem=a_recv.at[i, x],
@@ -198,7 +224,7 @@
     def h_copy(i, x, n):
         return pltpu.make_async_remote_copy(
             src_ref=hout.at[i, x],
-            dst_ref=hin.at[i, x],
+            dst_ref=entered.at[i, x],
             send_sem=h_send.at[i, x, n],
             recv_sem=h_recv.at[i, x],
             device_id={"mom": (mom + count - 1 - n) % count},
@@ -215,11 +241,6 @@
             device_id_type=MESH,
         )
 
-    def fill_parents(t, k):
-        parent = parent_ref[order[starts[t]]]
-        for x in range(cells):
-            comb[t * cells + x, 0, k] = f_parts[k][:, parent, x].astype(jnp.bfloat16)
-
     def send_parents(t, k):
         for x in range(cells):
             for d in range(1, sizes(x)[0]):
@@ -228,17 +249,32 @@
     odd = mom % 2 == 1
     ahead = 2
     small[0].wait()
-    order = classes(parent_ref)
+    for i, s in enumerate(classes(parent_ref)):
+        order_ref[i] = s
+    parent = parent_ref[order_ref[0]]
     for k in range(pieces):
         loads[k].wait()
-        fill_parents(0, k)
+        at = pl.ds(k * ROWS, ROWS)
+        for x in range(cells):
+            chosen = f_ref[:, 0, x, at, :]
+            for s in range(1, species):
+                chosen = jnp.where(parent == s, f_ref[:, s, x, at, :], chosen)
+            comb[x, 0, k] = chosen.astype(jnp.bfloat16)
         if k == 0:
             pl.semaphore_wait(barrier, count + 1)
         send_parents(0, k)
-    for t in range(1, slots):
-        for k in range(pieces):
-            fill_parents(t, k)
-            if t < ahead:
+
+    @pl.loop(1, slots)
+    def _(t):
+        parent = parent_ref[order_ref[first_of(t)]]
+
+        @pl.loop(0, pieces)
+        def _(k):
+            for x in range(cells):
+                comb[t * cells + x, 0, k] = f_ref[:, parent, x, rows(k), :].astype(jnp.bfloat16)
+
+            @pl.when(t < ahead)
+            def _():
                 send_parents(t, k)
 
     for copy in small[1:]:
@@ -302,27 +338,33 @@
     coef[2] = jnp.where(lane == radii - 1, 0.0, 0.5 * diff)
 
     for x in range(cells):
-        kept = jnp.ones((heights, radii), jnp.float32)
-        for p in range(bins):
-            part = 1.0 / (1.0 + 0.5 * rate_ref[p] * density_ref[x])
-            weight[p, x] = part
-            kept = kept * (1.0 - part)
-        keep[0, x] = kept
+        @pl.loop(0, pieces)
+        def _(k):
+            kept = jnp.ones((ROWS, radii), jnp.float32)
+            for p in range(bins):
+                part = 1.0 / (1.0 + 0.5 * rate_ref[p] * density_ref[x, rows(k), :])
+                weight[p, x, rows(k), :] = part
+                kept = kept * (1.0 - part)
+            keep[0, x, rows(k), :] = kept
 
     def keep_above():
         rate_copy().wait_recv()
         for x in range(cells):
-            kept = jnp.ones((heights, radii), jnp.float32)
-            for p in range(bins):
-                kept = kept * (1.0 - 1.0 / (1.0 + 0.5 * rates_in[pl.ds(p, 1), :] * density_ref[x]))
-            keep[1, x] = kept
+            @pl.loop(0, pieces)
+            def _(k):
+                dens = density_ref[x, rows(k), :]
+                kept = jnp.ones((ROWS, radii), jnp.float32)
+                for p in range(bins):
+                    kept = kept * (1.0 - 1.0 / (1.0 + 0.5 * rates_in[pl.ds(p, 1), :] * dens))
+                keep[1, x, rows(k), :] = kept
 
     @pl.when(mom >= count - 2)
     def _():
-        hin[...] = jnp.zeros_like(hin)
+        entered[...] = jnp.zeros_like(entered)
 
     def mix(t):
-        for k in range(pieces):
+        @pl.loop(0, pieces)
+        def _(k):
             for x in range(cells):
                 c = t * cells + x
                 n1, n2 = sizes(x)
@@ -334,43 +376,42 @@
                 for e in range(1, n2):
                     psend[c, e - 1, k] = sums[e].astype(jnp.bfloat16)
                     partial_copy(t, x, e, k).start()
-        if t + ahead < slots:
-            for k in range(pieces):
+
+        @pl.when(t + ahead < slots)
+        def _():
+            @pl.loop(0, pieces)
+            def _(k):
                 send_parents(t + ahead, k)
 
     def source(t):
-        for k in range(pieces):
-            at = pl.ds(k * ROWS, ROWS)
+        @pl.loop(0, pieces)
+        def _(k):
             for x in range(cells):
                 c = t * cells + x
                 n2 = sizes(x)[1]
                 for e in range(1, n2):
                     partial_copy(t, x, e, k).wait_recv()
 
-                @pl.loop(0, bins)
-                def _(p):
-                    value = own_part[c, k, p]
+                @pl.loop(first_of(t), first_of(t + 1))
+                def _(i):
+                    total = f_ref[:, order_ref[i], x, rows(k), :] + own_part[c, k]
                     for e in range(1, n2):
-                        value = value + precv[c, e - 1, k, p].astype(jnp.float32)
-                    for i in range(starts[t], starts[t] + kids[t]):
-                        total = f_parts[k][p, order[i], x] + value
-                        acc[i * cells + x, p, at, :] = total
-                        rounded = total.astype(jnp.bfloat16)
-                        if x == 0:
-                            faces_out[i, 0, k, p] = rounded
-                        if x == cells - 1:
-                            faces_out[i, 1, k, p] = rounded
-
-                for i in range(starts[t], starts[t] + kids[t]):
+                        total = total + precv[c, e - 1, k].astype(jnp.float32)
+                    acc[i * cells + x, :, rows(k), :] = total
+                    rounded = total.astype(jnp.bfloat16)
                     if x == 0:
+                        faces_out[i, 0, k] = rounded
                         face_copy(i, 0, k).start()
                     if x == cells - 1:
+                        faces_out[i, 1, k] = rounded
                         face_copy(i, 1, k).start()
 
     def diffuse(i):
-        for k in range(pieces):
+        @pl.loop(0, pieces)
+        def _(k):
             face_copy(i, 0, k).wait_recv()
             face_copy(i, 1, k).wait_recv()
+
         first = i * cells
         per = group // cells
 
@@ -410,6 +451,7 @@
                     total = 2.0 * acc[first + x, p, at, :] + carry
                     carry = total - total * weight[p, x, at, :]
                 below[i, x, at, :] = carry
+                below_out[i, x, at, :] = coded(carry)
 
     def send_below(i):
         @pl.when(odd)
@@ -417,79 +459,98 @@
             for x in range(cells):
                 below_copy(i, x).start()
 
-    def diffuse_slot(t, send):
-        @pl.loop(starts[t], starts[t] + kids[t])
-        def _(i):
-            diffuse(i)
-            if send:
-                send_below(i)
-
-    def relay(i):
+    def finish(i):
+        span = heights // 2
         for x in range(cells):
-            below_copy(i, x).wait_recv()
-
-            @pl.when(mom < count - 2)
+            @pl.when(odd)
             def _():
-                h_copy(i, x, 1).wait_recv()
-
-            entering = above[i, x] + keep[1, x] * hin[i, x]
-            hin[i, x] = entering
-            hout[i, x] = below[i, x] + keep[0, x] * entering
-
-            @pl.when(mom > 0)
+                @pl.when(mom < count - 1)
+                def _():
+                    h_copy(i, x, 0).wait_recv()
+
+                hin[x] = decoded(entered[i, x])
+
+            @pl.when(mom % 2 == 0)
             def _():
-                h_copy(i, x, 0).start()
-                h_copy(i, x, 1).start()
-
-    lag = (count - 1 - mom) // 2
+                below_copy(i, x).wait_recv()
+
+                @pl.when(mom < count - 2)
+                def _():
+                    h_copy(i, x, 1).wait_recv()
+
+                entering = decoded(above[i, x]) + keep[1, x] * decoded(entered[i, x])
+                hin[x] = entering
+                hout[i, x] = coded(below[i, x] + keep[0, x] * entering)
+
+                @pl.when(mom > 0)
+                def _():
+                    h_copy(i, x, 0).start()
+                    h_copy(i, x, 1).start()
+
+            @pl.loop(0, 2)
+            def _(k):
+                at = pl.ds(pl.multiple_of(k * span, span), span)
+                carry = hin[x, at, :]
+                for p in range(bins - 1, -1, -1):
+                    settled = acc[i * cells + x, p, at, :]
+                    total = 2.0 * settled + carry
+                    both = total * weight[p, x, at, :]
+                    acc[i * cells + x, p, at, :] = both - settled
+                    carry = total - both
+
     early = species - kids[-1]
-    for i in range(slots + 1):
-        if i < slots:
+    held = sum(kids[: max(slots - 2, 0)])
+
+    @pl.loop(0, slots + 2)
+    def _(i):
+        @pl.when(i < slots)
+        def _():
             mix(i)
-        if 1 <= i:
-            source(i - 1)
-        if i >= 2:
-            diffuse_slot(i - 2, False)
-        if i == max(slots - 1, 0):
+
+        @pl.when(i == slots - 1)
+        def _():
             @pl.when(mom % 2 == 0)
             def _():
                 keep_above()
 
-        if i == slots - 1:
-            @pl.loop(0, sum(kids[: max(slots - 2, 0)]))
-            def _(i):
-                send_below(i)
-        if i == slots:
-            @pl.loop(sum(kids[: max(slots - 2, 0)]), early)
-            def _(i):
-                send_below(i)
-
-    @pl.when((mom % 2 == 0) & (lag == 0))
-    def _():
-        @pl.loop(0, early)
-        def _(i):
-            relay(i)
-
-    diffuse_slot(slots - 1, True)
-
-    @pl.when((mom % 2 == 0) & (lag > 0))
-    def _():
-        @pl.loop(0, early)
-        def _(i):
-            relay(i)
-
-    @pl.when(mom % 2 == 0)
-    def _():
-        @pl.loop(early, species)
-        def _(i):
-            relay(i)
+        @pl.when((i >= 1) & (i < slots + 1))
+        def _():
+            source(i - 1)
+
+        @pl.when((i == slots + 1) & (mom >= count - 2))
+        def _():
+            @pl.loop(0, early)
+            def _(j):
+                finish(j)
+
+        @pl.when(i >= 2)
+        def _():
+            @pl.loop(first_of(i - 2), first_of(i - 1))
+            def _(j):
+                diffuse(j)
+
+                @pl.when(i >= slots)
+                def _():
+                    send_below(j)
+
+        @pl.when(i == slots - 1)
+        def _():
+            @pl.loop(0, held)
+            def _(j):
+                send_below(j)
+
+    @pl.loop(jnp.where(mom >= count - 2, early, 0), species)
+    def _(j):
+        finish(j)
 
     @pl.when(odd)
     def _():
         rate_copy().wait_send()
 
-    for t in range(slots):
-        for k in range(pieces):
+    @pl.loop(0, slots)
+    def _(t):
+        @pl.loop(0, pieces)
+        def _(k):
             for x in range(cells):
                 for d in range(1, sizes(x)[0]):
                     parent_copy(t, x, d, k).wait_send()
@@ -498,55 +559,32 @@
 
     @pl.loop(0, species)
     def _(i):
-        for k in range(pieces):
+        @pl.loop(0, pieces)
+        def _(k):
             face_copy(i, 0, k).wait_send()
             face_copy(i, 1, k).wait_send()
+
         for x in range(cells):
             @pl.when(odd)
             def _():
                 below_copy(i, x).wait_send()
 
-            @pl.when(odd & (mom < count - 1))
-            def _():
-                h_copy(i, x, 0).wait_recv()
-
             @pl.when((mom % 2 == 0) & (mom > 0))
             def _():
                 h_copy(i, x, 0).wait_send()
                 h_copy(i, x, 1).wait_send()
 
 
-def solve_kernel(
-    settled_ref, hin_ref, weight_ref, parent_hbm, out_hbm, done, parent_ref, in_sem, out_sem
-):
-    bins, cells, heights, radii = weight_ref.shape
-    species = parent_ref.shape[0]
-    span = heights // 2
-    load = pltpu.make_async_copy(parent_hbm, parent_ref, in_sem)
-    load.start()
-    order = None
-    copies = []
-    for i in range(species):
-        for x in range(cells):
-            n = i * cells + x
-
-            @pl.loop(0, 2)
-            def _(k):
-                at = pl.ds(pl.multiple_of(k * span, span), span)
-                carry = hin_ref[i, x, at, :]
-                for p in range(bins - 1, -1, -1):
-                    settled = settled_ref[n, p, at, :]
-                    total = 2.0 * settled + carry
-                    both = total * weight_ref[p, x, at, :]
-                    done[n, p, at, :] = both - settled
-                    carry = total - both
-
-            if order is None:
-                load.wait()
-                order = classes(parent_ref)
-            copy = pltpu.make_async_copy(done.at[n], out_hbm.at[:, order[i], x], out_sem.at[n])
-            copy.start()
-            copies.append(copy)
+def place_kernel(done, parent_ref, out_hbm, out_sem):
+    species, cells = out_hbm.shape[1:3]
+    order = classes(parent_ref)
+    copies = [
+        pltpu.make_async_copy(done.at[i * cells + x], out_hbm.at[:, order[i], x], out_sem.at[i, x])
+        for i in range(species)
+        for x in range(cells)
+    ]
+    for copy in copies:
+        copy.start()
     for copy in copies:
         copy.wait()
 
@@ -574,21 +612,18 @@
     most = max(nx, ny)
     group = cells * max(1, 256 // (heights * cells))
     dma = pltpu.SemaphoreType.DMA
-    vmem = pl.BlockSpec(memory_space=pltpu.VMEM)
-    hbm = pl.BlockSpec(memory_space=pltpu.HBM)
-    stay = functools.partial(pltpu.with_memory_space_constraint, memory_space=pltpu.HBM)
     tall, broad = ny * bins * ROWS, nx * bins * ROWS
-    settled, entering, weight = pl.pallas_call(
+    args = (
+        spectra, production, bin_group, parent_of, diffusivity, height_inverse, loss_rate, density
+    )
+    done = pl.pallas_call(
         functools.partial(step_kernel, ny, nx, kids),
-        out_shape=[
-            jax.ShapeDtypeStruct((species * cells,) + block, jnp.float32),
-            jax.ShapeDtypeStruct((species, cells) + plane, jnp.float32),
-            jax.ShapeDtypeStruct((bins, cells) + plane, jnp.float32),
-        ],
-        in_specs=[hbm] * 8,
-        out_specs=[vmem, vmem, vmem],
+        out_shape=jax.ShapeDtypeStruct((species * cells,) + block, jnp.float32),
+        in_specs=[HBM] * len(args),
+        out_specs=VMEM,
         scratch_shapes=[
-            [pltpu.VMEM((bins, species, cells, ROWS, radii), jnp.float32) for _ in range(pieces)],
+            pltpu.VMEM(spectra.shape, jnp.float32),
+            pltpu.SMEM(parent_of.shape, jnp.int32),
             pltpu.SMEM(parent_of.shape, jnp.int32),
             pltpu.SMEM(bin_group.shape, jnp.int32),
             pltpu.VMEM(production.shape, jnp.bfloat16),
@@ -603,8 +638,12 @@
             pltpu.VMEM((species, 2) + split, jnp.bfloat16),
             pltpu.VMEM((species, 2) + split, jnp.bfloat16),
             pltpu.VMEM((species, cells) + plane, jnp.float32),
-            pltpu.VMEM((species, cells) + plane, jnp.float32),
-            pltpu.VMEM((species, cells) + plane, jnp.float32),
+            pltpu.VMEM((species, cells) + plane, jnp.bfloat16),
+            pltpu.VMEM((species, cells) + plane, jnp.bfloat16),
+            pltpu.VMEM((species, cells) + plane, jnp.bfloat16),
+            pltpu.VMEM((cells,) + plane, jnp.float32),
+            pltpu.VMEM((species, cells) + plane, jnp.bfloat16),
+            pltpu.VMEM((bins, cells) + plane, jnp.float32),
             pltpu.VMEM((2, cells) + plane, jnp.float32),
             pltpu.VMEM((max(bins, 8), radii), jnp.float32),
             pltpu.VMEM((max(bins, 8), radii), jnp.float32),
@@ -628,38 +667,37 @@
             dma,
         ],
         compiler_params=pltpu.CompilerParams(
-            collective_id=which, has_side_effects=True, vmem_limit_bytes=40 * 1024 * 1024
+            collective_id=which, has_side_effects=True, vmem_limit_bytes=36 * 1024 * 1024
         ),
-    )(*(stay(a) for a in (
-        spectra, production, bin_group, parent_of, diffusivity, height_inverse, loss_rate, density
-    )))
+    )(*map(stay, args))
+    return place(done, parent_of, spectra)
+
+
+def place(done, parent_of, spectra):
+    species, cells = spectra.shape[1:3]
+    dma = pltpu.SemaphoreType.DMA
     return pl.pallas_call(
-        solve_kernel,
-        out_shape=jax.ShapeDtypeStruct(spectra.shape, jnp.float32),
-        in_specs=[vmem, vmem, vmem, hbm],
-        out_specs=hbm,
-        scratch_shapes=[
-            pltpu.VMEM((species * cells,) + block, jnp.float32),
-            pltpu.SMEM(parent_of.shape, jnp.int32),
-            dma,
-            dma((species * cells,)),
-        ],
+        place_kernel,
+        out_shape=pltpu.HBM(spectra.shape, jnp.float32),
+        in_specs=[VMEM, pl.BlockSpec(memory_space=pltpu.SMEM)],
+        out_specs=HBM,
+        scratch_shapes=[dma((species, cells))],
         compiler_params=pltpu.CompilerParams(vmem_limit_bytes=16 * 1024 * 1024),
-    )(settled, entering, weight, stay(parent_of))
+    )(done, parent_of)
 
 
 def step(ny, nx, *args):
     parent_of = args[3]
     species = parent_of.shape[0]
-    single = (1,) * species
-    if species != 4:
-        return local(ny, nx, 0, single, *args)
-    pairs = jnp.sum((parent_of[:, None] == parent_of[None, :]).astype(jnp.int32))
-    which = jnp.where(pairs > 8, 0, jnp.where(pairs > 6, 1, jnp.where(pairs > 4, 2, 3)))
-    forms = ((3, 1), (2, 2), (2, 1, 1), single)
-    return lax.switch(
-        which, [functools.partial(local, ny, nx, n, kids) for n, kids in enumerate(forms)], *args
-    )
+    forms = ((1,) * species,)
+    if species == 4:
+        forms += ((2, 1, 1), (2, 2), (3, 1))
+    kernels = [functools.partial(local, ny, nx, n, kids) for n, kids in enumerate(forms)]
+    if species == 4:
+        later = np.triu(np.ones((species, species), np.bool_), 1)
+        same = (parent_of[:, None] == parent_of[None, :]) & later
+        return lax.switch(jnp.sum(same.astype(jnp.int32)), kernels, *args)
+    return kernels[0](*args)
 
 
 def solution(mesh):

time: 63.9 us -> 59.8 us (0.936)
  local copies, waits for them, and re-layouts: 2.01 us -> 0.01 us
  between operations: 1.97 us -> 0.65 us
  Pallas kernels: 58.4 us -> 57.5 us
    unnamed x2 -> x0, local copies, waits for them, and re-layouts: 2.01 us -> none
    pallas_call x2, Pallas kernels: 58.4 us -> 57.5 us  [the longest x1 54.9 us: local(): pl.pallas_call(functools.partial(step_kernel, ny, nx, kids), out_shape=ja...]
where the time goes in v2:
time: 59.8 us; the launch traced here: 59.7 us
  Pallas kernels  57.5 us (96%)
  other arithmetic  1.44 us (2%)
  between operations  0.65 us (1%)
    pallas_call x1, Pallas kernels, local(): pl.pallas_call(functools.partial(step_kernel, ny, nx, kids), out_shape=ja...  54.9 us
    pallas_call x1, Pallas kernels, place(): pl.pallas_call(place_kernel, out_shape=pltpu.HBM(spectra.shape, jnp.float...  2.65 us
    reduce_sum x1, other arithmetic, step(): return lax.switch(jnp.sum(same.astype(jnp.int32)), kernels, *args)  1.44 us

profile of v2, /device:TPU:1, one launch (start us, length us, event | category | flops | bytes accessed | tf_op | source)
XLA Modules:
  0.0 59.7 jit_solution(14375365721607280481)
XLA Ops:
  0.0 1.4 %convert_reduce_fusion = s32[]{:T(128)} fusion(pred[4,4]{1,0:T(4,128)(4,1)} %constant.6.clone, s32[4]{0:T(128)} %param.16), kind=kLoop, calls=%fused_computation | loop fusion | flops 63 | bytes 36 | tf_op jit(solution)/shard_map/reduce_sum | solution.py:699
  2.1 57.6 %conditional.1 = (f32[8,4,2,64,256]{4,3,2,1,0:T(8,128)}) conditional(s32[]{:T(128)} %clamp.3, (f32[8,4,2,64,256]{4,3,2,1,0:T(8,128)}, bf16[32,32]{1,0:T(8,128)(2,1)}, s32[32]{0:T(128)}, s32[4]{0:T(128)}, f32[64,256]{1,0:T(8,128)}, /*index=5*/f32[64,64]{1,0:T(8,128)}, f32[8]{0:T(128)}, ...), branch_computations={%region_1.0_spmd, %region_2.0_spmd, %region_3.0_spmd, %region_4.0_... | conditional | bytes 100 | solution.py:699
  2.1 0.0 copy-start.1
  2.1 54.9 %branch_1_fun.2.done = f32[8,8,64,256]{3,2,1,0:T(8,128)S(1)} custom-call(f32[8,4,2,64,256]{4,3,2,1,0:T(8,128)} %get-tuple-element.82.f_hbm, bf16[32,32]{1,0:T(8,128)(2,1)} %get-tuple-element.83.production_hbm, s32[32]{0:T(128)} %get-tuple-element.84.group_hbm, s32[4]{0:T(128)} %get-tuple-element.85.parent_hbm.parent_ref, ...), custom_call_target="tpu_custom_call" | custom-call | tf_op jit(solution)/shard_map/cond/branch_1_fun/pallas_call | solution.py:619
  57.0 0.0 copy-done.1
  57.0 2.6 %branch_1_fun.3 = f32[8,4,2,64,256]{4,3,2,1,0:T(8,128)} custom-call(f32[8,8,64,256]{3,2,1,0:T(8,128)S(1)} %branch_1_fun.2.done, s32[4]{0:T(128)S(1)} %copy-done.1), custom_call_target="tpu_custom_call" | custom-call | tf_op jit(solution)/shard_map/cond/branch_1_fun/pallas_call | solution.py:679
Async XLA Ops:
  2.1 54.9 %copy-start.1 = (s32[4]{0:T(128)S(1)}, s32[4]{0:T(128)}, u32[]{:S(2)}) copy-start(s32[4]{0:T(128)} %get-tuple-element.85.parent_hbm.parent_ref) | copy-start | bytes 52 | tf_op jit(solution)/shard_map/cond
